TPU v7x, 512 devices: a whole 4x4x16 slice. The times are simulated.
512 devices in a mesh: ctx: 32 (over z, core), head: 8 (over y, x_lo), dp: 2 (over x_hi).
Axes of the slice: x: 4 (x_hi: 2, x_lo: 2; x = x_hi * 2 + x_lo), y: 4, z: 16, core: 2. Of those that a mesh axis runs over, the one named last changes fastest.
Arguments:
- queries: bfloat16 [16384, 4096], P(('dp', 'ctx'), 'head'), parts along dimension 0, may hold values from -12 to 12
- keys_values: bfloat16 [2, 16384, 1024], P(None, ('dp', 'ctx'), 'head'), parts along dimension 1, may hold values from -12 to 12
- positions: int32 [16384], P(('dp', 'ctx')), parts along dimension 0, may hold values from 0 to 4096, as said below
- offsets: int32 [16], P('dp'), parts along dimension 0, may hold values from 0 to 8190, as said below
- w_out: bfloat16 [4096, 4096], P('head'), may hold values from -0.375 to 0.375
Outputs:
- mixed: bfloat16 [16384, 4096], P(('dp', 'ctx'), 'head'), parts along dimension 0
There are 2 independent parts, one for each index of `dp`. A program takes and returns all parts, laid end to end along the dimension named above; an argument that names none is the same for every part. Nothing has to cross between parts.
Inputs may be any that keep to these rules, and one draw needn't show every extreme that they name: offsets[0] = 0 and the offsets rise strictly; the first document holds exactly 4097 tokens and every later one two or more. positions[t] = t minus the largest offset not above t.
All inputs are finite; a program needn't handle non-finite values.
Results may differ from a plain program's by a relative error of at most 0.02.
Values may be sent and summed in bfloat16 or wider, within the bound.
A program may use at most 128 MiB of HBM per device.

v0:
```python
import math
import jax
import jax.numpy as jnp
from jax import lax
from jax.sharding import PartitionSpec as P

HD = 128
ROPE_BASE = 500000.0
STRETCH = 16.0
ANCHOR_LENGTH = 8192.0
BETA_FAST = 32.0
BETA_SLOW = 1.0
MAGNITUDE = 0.1 * math.log(16.0) + 1.0
NEGATIVE = -1e30


def tables(positions, width):
    half = width // 2
    index = jnp.arange(half, dtype=jnp.float32)
    base_freq = jnp.exp(index * (-2.0 * math.log(ROPE_BASE) / width))
    ratio = base_freq * (ANCHOR_LENGTH / (2.0 * math.pi))
    ramp = jnp.clip((ratio - BETA_SLOW) / (BETA_FAST - BETA_SLOW), 0.0, 1.0)
    freq = base_freq * (1.0 - ramp) / STRETCH + base_freq * ramp
    angle = positions.astype(jnp.float32)[:, None] * freq[None, :]
    return (jnp.cos(angle) * MAGNITUDE, jnp.sin(angle) * MAGNITUDE)


def rotate(field, cosine, sine):
    half = field.shape[-1] // 2
    first = field[..., :half]
    second = field[..., half:]
    cos_rows = cosine[:, None, :]
    sin_rows = sine[:, None, :]
    return jnp.concatenate(
        [first * cos_rows - second * sin_rows, second * cos_rows + first * sin_rows], axis=-1
    )


def shards(queries, keys_values, positions, offsets, w_out):
    rows = queries.shape[0]
    heads_here = w_out.shape[0] // HD
    cosine, sine = tables(positions, HD)
    rot_queries = (
        rotate(queries.reshape(rows, heads_here, HD).astype(jnp.float32), cosine, sine)
        * HD ** (-0.5)
    ).astype(jnp.bfloat16)
    rot_keys = (
        rotate(keys_values[0].reshape(rows, 1, HD).astype(jnp.float32), cosine, sine)
        .reshape(rows, HD)
        .astype(jnp.bfloat16)
    )
    moving = jnp.stack([rot_keys, keys_values[1]])
    first = lax.axis_index("ctx") * rows
    query_index = first + jnp.arange(rows, dtype=jnp.int32)
    starts = jnp.max(
        jnp.where(offsets[None, :] <= query_index[:, None], offsets[None, :], 0), axis=1
    )
    piece = lax.all_gather(moving, "ctx", axis=1, tiled=True)
    key_rows = piece[0]
    value_rows = piece[1]
    count = key_rows.shape[0]
    key_index = jnp.arange(count, dtype=jnp.int32)
    visible = (
        (key_index[None, :] <= query_index[:, None]) & (key_index[None, :] >= starts[:, None])
    )[:, None, :]
    scores = jnp.einsum("qhd,kd->qhk", rot_queries, key_rows, preferred_element_type=jnp.float32)
    peak = jnp.full((rows, heads_here), NEGATIVE, jnp.float32)
    new_peak = jnp.maximum(peak, jnp.max(jnp.where(visible, scores, NEGATIVE), axis=2))
    expo = jnp.where(visible, jnp.exp(scores - new_peak[..., None]), 0.0)
    total = jnp.sum(expo, axis=2)
    accum = jnp.einsum(
        "qhk,kd->qhd", expo.astype(jnp.bfloat16), value_rows, preferred_element_type=jnp.float32
    )
    result = (new_peak, total, accum)
    peak, total, accum = result
    attended = (accum / total[..., None]).astype(jnp.bfloat16).reshape(rows, heads_here * HD)
    partial_value = jnp.dot(attended, w_out, preferred_element_type=jnp.float32)
    return lax.psum_scatter(
        partial_value.astype(jnp.bfloat16), "head", scatter_dimension=1, tiled=True
    )


def solution(mesh):
    in_specs = (
        P(("dp", "ctx"), "head"),
        P(None, ("dp", "ctx"), "head"),
        P(("dp", "ctx")),
        P("dp"),
        P("head", None),
    )
    out_specs = P(("dp", "ctx"), "head")
    return jax.shard_map(shards, mesh=mesh, in_specs=in_specs, out_specs=out_specs, check_vma=False)
```

profile of v0, /device:TPU:1, one launch (start us, length us, event | category | flops | bytes accessed | tf_op | source)
XLA Modules:
  0.0 207.3 jit_solution(4234741551339588215)
XLA Ops:
  6.5 0.0 all-gather.2.cloned.1.call-start
  6.6 0.7 convert_element_type.48
  7.2 0.9 fusion.32
  8.1 0.1 copy.25
  8.3 0.1 copy.26
  8.4 0.3 fusion.22
  8.7 0.7 pad_maximum_fusion
  9.4 0.0 all-gather.2.cloned.1.call-update
  9.4 0.0 reduce-scatter.2.cloned.1.call-start
  9.5 1.1 copy.15
  10.6 0.2 copy.24
  10.8 0.2 copy.23
  11.0 0.7 select_reduce_fusion.1
  11.8 0.5 fusion.16
  12.3 0.1 multiply_subtract_fusion
  12.4 2.0 fusion.5
  14.4 80.9 %all-gather.2.cloned.1.call-done = bf16[2,8192,128]{1,2,0:T(8,128)(2,1)} async-done(((bf16[2,256,128]{1,2,0:T(8,128)(2,1)}), bf16[2,8192,128]{1,2,0:T(8,128)(2,1)}) %all-gather.2.cloned.1.call-update) | async-done | bytes 4194320 | tf_op jit(solution)/shard_map/all_gather | solution.py:58
  95.4 15.2 %select_reduce_fusion = (f32[256,4]{0,1:T(4,128)S(1)}, f32[256,4,8192]{2,0,1:T(8,128)}) fusion(pred[256,8192]{1,0:T(8,128)(4,1)S(1)} %fusion.5, bf16[2,8192,128]{1,2,0:T(8,128)(2,1)} %all-gather.2.cloned.1.call-done, f32[256,4,64]{2,0,1:T(8,128)S(1)} %get-tuple-element.6, f32[256,4,64]{2,0,1:T(8,128)S(1)} %get-tuple-element.5), kind=kOutput, calls=%fused_computation.1 | convolution fusion | flops 2164653056 | bytes 38277120 | tf_op jit(solution)/shard_map/qhd,kd->qhk/dot_general | solution.py:66
  110.5 14.7 %fusion = f32[256,4]{0,1:T(4,128)S(1)} fusion(f32[256,4,8192]{2,0,1:T(8,128)} %get-tuple-element.16, f32[256,4]{0,1:T(4,128)S(1)} %broadcast_maximum_fusion, pred[256,8192]{1,0:T(8,128)(4,1)S(1)} %fusion.5), kind=kLoop, calls=%fused_computation.2 | loop fusion | flops 25164800 | bytes 35659776 | tf_op jit(solution)/shard_map/reduce_sum | solution.py:70
  125.2 14.3 %fusion.10 = bf16[256,4,128]{0,2,1:T(8,128)(2,1)S(1)} fusion(bf16[2,8192,128]{1,2,0:T(8,128)(2,1)} %all-gather.2.cloned.1.call-done, f32[256,4,8192]{2,0,1:T(8,128)} %get-tuple-element.16, f32[256,4]{0,1:T(4,128)S(1)} %broadcast_maximum_fusion, pred[256,8192]{1,0:T(8,128)(4,1)S(1)} %fusion.5, f32[256,4]{0,1:T(4,128)S(1)} %fusion), kind=kOutput, calls=%fused_computation.14 | convolution fusion | flops 2172911616 | bytes 38019072 | tf_op jit(solution)/shard_map/qhk,kd->qhd/dot_general | solution.py:71
  139.5 4.8 %convolution_convert_fusion = bf16[256,4096]{1,0:T(8,128)(2,1)} fusion(bf16[256,512]{0,1:T(8,128)(2,1)S(1)} %bitcast.26, bf16[512,4096]{1,0:T(8,128)(2,1)} %param.9), kind=kOutput, calls=%fused_computation.9 | convolution fusion | flops 1074790400 | bytes 6553600 | tf_op jit(solution)/shard_map/dot_general | solution.py:77
  144.3 0.0 reduce-scatter.2.cloned.1.call-update
  144.3 56.2 %reduce-scatter.2.cloned.1.call-done = bf16[256,512]{1,0:T(8,128)(2,1)} async-done(((bf16[256,4096]{1,0:T(8,128)(2,1)}), bf16[256,512]{1,0:T(8,128)(2,1)}) %reduce-scatter.2.cloned.1.call-update) | async-done | bytes 262160 | tf_op jit(solution)/shard_map/reduce_scatter | solution.py:78
  (6 shorter events, 0.1 us)
Async XLA Ops:
  6.5 88.8 %all-gather.2.cloned.1.call-start = ((), (), s32[]{:S(2)}) async-start(), calls=%async_computation.1 | async-start | bytes 4325376 | tf_op jit(solution)/shard_map/all_gather | solution.py:58
  9.4 191.1 %reduce-scatter.2.cloned.1.call-start = ((), (), s32[]{:S(2)}) async-start(), calls=%async_computation.2 | async-start | bytes 2359296 | tf_op jit(solution)/shard_map/reduce_scatter | solution.py:78
Sparse Core Ops, SparseCore 0:
  9.5 85.7 all-gather.1
  144.4 56.0 reduce-scatter.1
where the time goes:
time: 208 us; the launch traced here: 207 us
  waiting for transfers between devices  137 us (66%)
  matrix products  34.2 us (16%)
  other arithmetic  19.8 us (10%)
  between operations  13.5 us (6%)
  local copies, waits for them, and re-layouts  2.61 us (1%)
    all_gather x1, waiting for transfers between devices, shards(): piece = lax.all_gather(moving, 'ctx', axis=1, tiled=True)  80.9 us
    reduce_scatter x1, waiting for transfers between devices, shards(): lax.psum_scatter(partial_value.astype(jnp.bfloat16), 'head', scatter_dime...  56.2 us
    dot_general x1, matrix products, shards(): jnp.einsum('qhd,kd->qhk', rot_queries, key_rows, preferred_element_type=j...  15.2 us
    reduce_sum x1, other arithmetic, shards(): total = jnp.sum(expo, axis=2)  14.7 us
    dot_general x1, matrix products, shards(): jnp.einsum('qhk,kd->qhd', expo.astype(jnp.bfloat16), value_rows, preferre...  14.3 us
    dot_general x1, matrix products, shards(): partial_value = jnp.dot(attended, w_out, preferred_element_type=jnp.float32)  4.81 us
  transfers between devices with their start and end apart: 2, of which 2 were waited for; matrix products, arithmetic and copies ran while one was open for 2% of the time, Pallas kernels for 0%

commit v1 on v0

--- a/solution.py
+++ b/solution.py
@@ -12,6 +12,13 @@
 BETA_SLOW = 1.0
 MAGNITUDE = 0.1 * math.log(16.0) + 1.0
 NEGATIVE = -1e30
+
+
+def keep_up_strips_all(point, device_axis):
+    tall = jnp.concatenate(
+        lax.all_to_all(jnp.stack([point] * lax.axis_size(device_axis), 0), device_axis, 0, 0), 1
+    )
+    return tall
 
 
 def tables(positions, width):
@@ -55,7 +62,7 @@
     starts = jnp.max(
         jnp.where(offsets[None, :] <= query_index[:, None], offsets[None, :], 0), axis=1
     )
-    piece = lax.all_gather(moving, "ctx", axis=1, tiled=True)
+    piece = keep_up_strips_all(moving, "ctx")
     key_rows = piece[0]
     value_rows = piece[1]
     count = key_rows.shape[0]

time: 208 us -> 330 us (1.59)
  waiting for transfers between devices: 137 us -> 239 us
  starting transfers between devices: 0.04 us -> 17 us
  local copies, waits for them, and re-layouts: 2.61 us -> 8.7 us
    all_to_all x0 -> x1, waiting for transfers between devices: none -> 180 us  [keep_up_strips_all(): lax.all_to_all(jnp.stack([point] * lax.axis_size(device_axis), 0), device...]
    all_gather x1 -> x0, waiting for transfers between devices: 80.9 us -> none  [shards(): piece = lax.all_gather(moving, 'ctx', axis=1, tiled=True)]
    all_to_all x0 -> x1, starting transfers between devices: none -> 16.9 us  [keep_up_strips_all(): lax.all_to_all(jnp.stack([point] * lax.axis_size(device_axis), 0), device...]
    slice x0 -> x1, local copies, waits for them, and re-layouts: none -> 3.92 us  [shards(): key_rows = piece[0]]
  transfers between devices with their start and end apart: 2 -> 2, of which waited for: 2 -> 2; matrix products, arithmetic and copies ran while one was open for 2% -> 1% of each run, Pallas kernels for 0% -> 0%
where the time goes in v1:
time: 330 us; the launch traced here: 329 us
  waiting for transfers between devices  239 us (72%)
  matrix products  32.7 us (10%)
  other arithmetic  18.4 us (6%)
  starting transfers between devices  17 us (5%)
  between operations  13.6 us (4%)
  local copies, waits for them, and re-layouts  8.7 us (3%)
    all_to_all x1, waiting for transfers between devices, keep_up_strips_all(): lax.all_to_all(jnp.stack([point] * lax.axis_size(device_axis), 0), device...  180 us
    reduce_scatter x1, waiting for transfers between devices, shards(): lax.psum_scatter(partial_value.astype(jnp.bfloat16), 'head', scatter_dime...  59.1 us
    all_to_all x1, starting transfers between devices, keep_up_strips_all(): lax.all_to_all(jnp.stack([point] * lax.axis_size(device_axis), 0), device...  16.9 us
    reduce_sum x1, other arithmetic, shards(): total = jnp.sum(expo, axis=2)  14.7 us
    dot_general x1, matrix products, shards(): jnp.einsum('qhk,kd->qhd', expo.astype(jnp.bfloat16), value_rows, preferre...  14.5 us
    dot_general x1, matrix products, shards(): jnp.einsum('qhd,kd->qhk', rot_queries, key_rows, preferred_element_type=j...  13.3 us
  transfers between devices with their start and end apart: 2, of which 2 were waited for; matrix products, arithmetic and copies ran while one was open for 1% of the time, Pallas kernels for 0%

profile of v1, /device:TPU:1, one launch (start us, length us, event | category | flops | bytes accessed | tf_op | source)
XLA Modules:
  0.0 329.3 jit_solution(3566332955605618457)
XLA Ops:
  6.6 0.7 convert_element_type.48
  7.2 0.9 fusion.33
  8.1 0.1 copy.29
  8.3 0.1 copy.30
  8.4 0.3 fusion.22
  8.7 0.1 copy.24
  8.9 3.0 stack.5
  11.9 16.9 %all-to-all-start = ((bf16[32,2,256,128]{3,2,1,0:T(8,128)(2,1)}), bf16[32,2,256,128]{3,2,1,0:T(8,128)(2,1)}, u32[]{:S(2)}, u32[]{:S(2)}) async-start(bf16[32,2,256,128]{3,2,1,0:T(8,128)(2,1)} %stack.5), calls=%async_computation | async-start | bytes 8388608 | tf_op jit(solution)/shard_map/all_to_all | solution.py:19
  28.8 0.0 reduce-scatter.2.cloned.1.call-start
  28.9 0.1 copy.19
  29.1 0.2 copy.28
  29.3 0.2 copy.27
  29.5 0.1 select_reduce_fusion.1
  29.6 0.5 fusion.16
  30.1 0.1 multiply_subtract_fusion
  30.2 2.0 fusion.5
  32.2 179.8 %all-to-all-done = bf16[32,2,256,128]{3,2,1,0:T(8,128)(2,1)} async-done(((bf16[32,2,256,128]{3,2,1,0:T(8,128)(2,1)}), bf16[32,2,256,128]{3,2,1,0:T(8,128)(2,1)}, u32[]{:S(2)}, u32[]{:S(2)}) %all-to-all-start) | async-done | bytes 4194336 | tf_op jit(solution)/shard_map/all_to_all | solution.py:19
  212.1 3.9 %fusion.31 = (bf16[1,32,256,128]{3,2,0,1:T(8,128)(2,1)S(1)}, bf16[1,32,256,128]{3,2,0,1:T(8,128)(2,1)}) fusion(bf16[2,32,256,128]{3,2,0,1:T(8,128)(2,1)} %bitcast.5), kind=kLoop, calls=%fused_computation.44 | loop fusion | bytes 8388608 | tf_op jit(solution)/shard_map/slice | solution.py:66
  216.0 13.3 %select_reduce_fusion = (f32[256,4]{0,1:T(4,128)S(1)}, f32[256,4,8192]{2,0,1:T(8,128)}) fusion(pred[256,8192]{1,0:T(8,128)(4,1)S(1)} %fusion.5, bf16[8192,128,1]{1,0,2:T(8,128)(2,1)S(1)} %bitcast.20, f32[256,4,64]{2,0,1:T(8,128)S(1)} %get-tuple-element.8, f32[256,4,64]{2,0,1:T(8,128)S(1)} %get-tuple-element.7), kind=kOutput, calls=%fused_computation.1 | convolution fusion | flops 2164653056 | bytes 38277120 | tf_op jit(solution)/shard_map/qhd,kd->qhk/dot_general | solution.py:73
  229.3 14.7 %fusion = f32[256,4]{0,1:T(4,128)S(1)} fusion(f32[256,4,8192]{2,0,1:T(8,128)} %get-tuple-element.18, f32[256,4]{0,1:T(4,128)S(1)} %broadcast_maximum_fusion, pred[256,8192]{1,0:T(8,128)(4,1)S(1)} %fusion.5), kind=kLoop, calls=%fused_computation.2 | loop fusion | flops 25164800 | bytes 35659776 | tf_op jit(solution)/shard_map/reduce_sum | solution.py:77
  244.0 14.5 %fusion.9 = bf16[256,4,128]{0,2,1:T(8,128)(2,1)S(1)} fusion(bf16[8192,128,1]{1,0,2:T(8,128)(2,1)} %bitcast.22, f32[256,4,8192]{2,0,1:T(8,128)} %get-tuple-element.18, f32[256,4]{0,1:T(4,128)S(1)} %broadcast_maximum_fusion, pred[256,8192]{1,0:T(8,128)(4,1)S(1)} %fusion.5, f32[256,4]{0,1:T(4,128)S(1)} %fusion), kind=kOutput, calls=%fused_computation.11 | convolution fusion | flops 2172911616 | bytes 38019072 | tf_op jit(solution)/shard_map/qhk,kd->qhd/dot_general | solution.py:78
  258.5 4.8 %convolution_convert_fusion = bf16[256,4096]{1,0:T(8,128)(2,1)} fusion(bf16[256,512]{0,1:T(8,128)(2,1)S(1)} %bitcast.23, bf16[512,4096]{1,0:T(8,128)(2,1)} %param.9), kind=kOutput, calls=%fused_computation.9 | convolution fusion | flops 1074790400 | bytes 6553600 | tf_op jit(solution)/shard_map/dot_general | solution.py:84
  263.3 0.0 reduce-scatter.2.cloned.1.call-update
  263.4 59.1 %reduce-scatter.2.cloned.1.call-done = bf16[256,512]{1,0:T(8,128)(2,1)} async-done(((bf16[256,4096]{1,0:T(8,128)(2,1)}), bf16[256,512]{1,0:T(8,128)(2,1)}) %reduce-scatter.2.cloned.1.call-update) | async-done | bytes 262160 | tf_op jit(solution)/shard_map/reduce_scatter | solution.py:85
  (11 shorter events, 0.1 us)
Async XLA Ops:
  11.9 17.0 %copy-start = (bf16[256,512]{1,0:T(8,128)(2,1)S(1)}, bf16[256,512]{1,0:T(8,128)(2,1)}, u32[]{:S(2)}) copy-start(bf16[256,512]{1,0:T(8,128)(2,1)} %param.5) | copy-start | bytes 786436
  11.9 17.6 %copy-start.1 = (s32[8]{0:T(128)S(1)}, s32[8]{0:T(128)}, u32[]{:S(2)}) copy-start(s32[8]{0:T(128)} %param.8) | copy-start | bytes 100
  11.9 200.2 %all-to-all-start = ((bf16[32,2,256,128]{3,2,1,0:T(8,128)(2,1)}), bf16[32,2,256,128]{3,2,1,0:T(8,128)(2,1)}, u32[]{:S(2)}, u32[]{:S(2)}) async-start(bf16[32,2,256,128]{3,2,1,0:T(8,128)(2,1)} %stack.5), calls=%async_computation | async-start | bytes 8388608 | tf_op jit(solution)/shard_map/all_to_all | solution.py:19
  28.8 293.6 %reduce-scatter.2.cloned.1.call-start = ((), (), s32[]{:S(2)}) async-start(), calls=%async_computation.2 | async-start | bytes 2359296 | tf_op jit(solution)/shard_map/reduce_scatter | solution.py:85
Sparse Core Ops, SparseCore 0:
  263.5 58.8 reduce-scatter.1
